TPU v7x, 256 devices: a whole 4x4x8 slice. The times are simulated.
256 devices in a mesh: gx: 16 (over x_hi, z), gy: 8 (over y, core), ta: 2 (over x_lo).
Axes of the slice: x: 4 (x_hi: 2, x_lo: 2; x = x_hi * 2 + x_lo), y: 4, z: 8, core: 2. Of those that a mesh axis runs over, the one named last changes fastest.
Arguments:
- whitened: float32 [2, 512, 16384], P(None, 'gx', ('gy', 'ta')), may hold values from -6 to 6
- factor_x: float32 [512, 512], P('gx'), as said below
- factor_y: float32 [256, 256], P(('gy', 'ta')), as said below
- factor_t: float32 [64, 64], replicated, as said below
- mark_loadings: float32 [2, 64], replicated, may hold values from -1 to 1
- mark_offsets: float32 [64], replicated, may hold values from -1.5 to 1.5
- exposure: float32 [512, 16384], P('gx', ('gy', 'ta')), may hold values from 0.3 to 3
- counts: int32 [64, 512, 16384], P(None, 'gx', ('gy', 'ta')), may hold values from 0 to 3
Outputs:
- gradient: float32 [2, 512, 16384], P(None, 'gx', ('gy', 'ta'))
Inputs may be any that keep to these rules, and one draw needn't show every extreme that they name: `factor_x`: A dense square matrix. `factor_y`: A dense square matrix. `factor_t`: A dense square matrix.
All inputs are finite; a program needn't handle non-finite values.
Results may differ from a plain program's by a relative error of at most 0.0003.
Values sent between devices are 32-bit elements; how exact they have to be, the bound alone decides.
A program may use at most 128 MiB of HBM per device.

v0:
```python
import math

import jax
import jax.numpy as jnp
from jax import lax
from jax.experimental import pallas as pl
from jax.experimental.pallas import tpu as pltpu
from jax.sharding import PartitionSpec as P

MESH = pl.DeviceIdType.MESH
F32 = jnp.float32
BF16 = jnp.bfloat16
LOG2E = math.log2(math.e)
N = 16
PIECE = 32
ROWS = N * PIECE
MARKS = 64
SHIFT = 8.0
GROUP = 64
Y_IN, Y_OUT, X_IN, X_OUT, BY_IN, BY_OUT, SUMS = range(7)
X_STEPS = sorted(
    [(z, x) for z in range(8) for x in range(2) if z or x], key=lambda s: -(min(s[0], 8 - s[0]) + 2 * s[1])
)
Y_STEPS = sorted(
    [(y, c, x) for y in range(4) for c in range(2) for x in range(2) if y or c or x],
    key=lambda s: -(min(s[0], 4 - s[0]) + s[2]),
)


def split(a):
    high = a.astype(BF16)
    return high, (a - high.astype(F32)).astype(BF16)


def dot(a, b, dims=((1,), (0,))):
    def one(left, right):
        return lax.dot_general(left, right, (dims, ((), ())), preferred_element_type=F32)

    return one(a[0], b[0]) + (one(a[0], b[1]) + one(a[1], b[0]))


def swap_halves(a):
    return pltpu.roll(a, 64, 1)


def kernel(
    load_hbm, off_hbm, w_hbm, fx_hbm, fy_hbm, ft_hbm, exp_hbm, counts_hbm, out_ref,
    load_ref, off_ref, w_v, exp_v, counts_v, sums_v, ft_v,
    fx_v, fx_parts, fxt_parts, fy_v, fyt_parts,
    t_v, send_v, recv_v, exp_send, exp_recv,
    local_sem, send_sem, recv_sem, exp_sem, fx_sem, fy_sem,
):
    gx = lax.axis_index("gx")
    gy = lax.axis_index("gy")
    ta = lax.axis_index("ta")
    j = gy * 2 + ta
    core = lax.rem(gy, 2)

    def x_peer(step):
        x = gx // 8
        k = (x + step[1] - 2 * x * step[1]) * 8 + lax.rem(gx + step[0], 8)
        return k, {"gx": k}

    def y_peer(step):
        y = lax.rem(gy // 2 + step[0], 4)
        a = y * 2 + (core + step[1] - 2 * core * step[1])
        b = ta + step[2] - 2 * ta * step[2]
        return a * 2 + b, {"gy": a, "ta": b}

    x_peers = [x_peer(step) for step in X_STEPS]
    y_peers = [y_peer(step) for step in Y_STEPS]

    loads = []
    for number, (source, target) in enumerate(
        (
            (w_hbm, w_v),
            (ft_hbm, ft_v),
            (fy_hbm, fy_v.at[j]),
            (fx_hbm.at[core], fx_v.at[gx, core]),
            (load_hbm, load_ref),
            (off_hbm, off_ref),
            (exp_hbm, exp_v),
            (counts_hbm, counts_v),
        )
    ):
        loads.append(pltpu.make_async_copy(source, target, local_sem.at[number]))
        loads[-1].start()

    barrier = pltpu.get_barrier_semaphore()
    for _, at in y_peers + x_peers:
        pl.semaphore_signal(barrier, inc=1, device_id=at, device_id_type=MESH)

    def push(source, target, sends, receives, at):
        pltpu.make_async_remote_copy(
            src_ref=source, dst_ref=target, send_sem=sends, recv_sem=receives, device_id=at, device_id_type=MESH
        ).start()

    def rows_of(k, piece=PIECE):
        return pl.ds(pl.multiple_of(k * piece, piece), piece)

    def exchange(phase, me, peers):
        for k, at in peers:
            push(send_v.at[phase, rows_of(k)], recv_v.at[phase, rows_of(me)], send_sem.at[phase], recv_sem.at[phase], at)
        recv_v[phase, rows_of(me), :] = send_v[phase, rows_of(me), :]

    def bytes_of(part, sem):
        pltpu.make_async_copy(part, part, sem).wait()

    def arrived(phase):
        bytes_of(recv_v.at[phase, pl.ds(0, ROWS - PIECE)], recv_sem.at[phase])

    def sent(phase):
        bytes_of(send_v.at[phase, pl.ds(0, ROWS - PIECE)], send_sem.at[phase])

    def low(rows):
        return lax.broadcasted_iota(jnp.int32, (rows, 128), 1) < 64

    def pack(first, second):
        half = low(first.shape[0])
        return jnp.where(half, first, swap_halves(second)), jnp.where(half, swap_halves(first), second)

    def lines(ref):
        found = []
        for g in range(8):
            found += pack(ref[0, :, g * 128 : g * 128 + 128], ref[1, :, g * 128 : g * 128 + 128])
        return jnp.concatenate(found, axis=0)

    def lines_to_columns(load, phase):
        for x in range(32):
            send_v[phase, pl.ds(x * 16, 16), :] = load(pl.ds(x, 16, stride=32))

    def y_mix(source, target, matrix):
        both = [
            jnp.concatenate([recv_v[source, pl.ds(k * PIECE + h * 16, 16), :] for k in range(N)], axis=0)
            for h in range(2)
        ]
        mixed = dot(matrix, split(jnp.concatenate(both, axis=1)))
        for k in range(N):
            for h in range(2):
                send_v[target, pl.ds(k * PIECE + h * 16, 16), :] = mixed[k * 16 : k * 16 + 16, h * 128 : h * 128 + 128]

    def sum_counts():
        for xt in range(4):
            xs = slice(xt * 8, xt * 8 + 8)

            def mark(m, total):
                tile = counts_v[m, xs, :].astype(F32)
                return total[0] + load_ref[0, m] * tile, total[1] + load_ref[1, m] * tile

            zero = jnp.zeros((8, 1024), F32)
            sums_v[0, xs, :], sums_v[1, xs, :] = lax.fori_loop(0, MARKS, mark, (zero, zero), unroll=4)

    for number in range(4):
        loads[number].wait()
    nothing = jnp.zeros((64, 64), F32)
    time = split(
        jnp.concatenate(
            [jnp.concatenate([ft_v[...], nothing], axis=1), jnp.concatenate([nothing, ft_v[...]], axis=1)], axis=0
        )
    )
    t_v[...] = dot(split(lines(w_v)), time, ((1,), (1,)))
    lines_to_columns(lambda rows: t_v[rows, :], Y_IN)

    pl.semaphore_wait(barrier, 2 * (N - 1))

    for _, at in y_peers:
        push(fy_v.at[j], fy_v.at[j], fy_sem.at[0], fy_sem.at[1], at)
    exchange(Y_IN, j, y_peers)
    for _, at in x_peers:
        push(fx_v.at[gx, core], fx_v.at[gx, core], fx_sem.at[0], fx_sem.at[1], at)

    for number in range(4, 8):
        loads[number].wait()
    for g in range(8):
        cols = slice(g * 128, g * 128 + 128)
        even, odd = pack(exp_v[0:16, cols], exp_v[16:32, cols])
        exp_send[g * 32 : g * 32 + 16, :] = even
        exp_send[g * 32 + 16 : g * 32 + 32, :] = odd
    for k, at in x_peers:
        push(exp_send.at[rows_of(k, 16)], exp_recv.at[rows_of(gx, 16)], exp_sem.at[0], exp_sem.at[1], at)
    exp_recv[rows_of(gx, 16), :] = exp_send[rows_of(gx, 16), :]

    sum_counts()
    send_v[SUMS] = lines(sums_v)
    exchange(SUMS, gx, x_peers)

    fy_part = fy_v.at[pl.ds(0, N - 1)]
    bytes_of(fy_part, fy_sem.at[1])
    fy = fy_v[...].reshape(256, 256)
    arrived(Y_IN)
    y_mix(Y_IN, Y_OUT, split(fy))
    exchange(Y_OUT, j, y_peers)
    fyt_parts[0], fyt_parts[1] = split(jnp.transpose(fy))
    arrived(Y_OUT)

    for y in range(N):
        send_v[X_IN, pl.ds(y * 32, 32), :] = recv_v[Y_OUT, pl.ds(y, 32, stride=16), :]
    exchange(X_IN, gx, x_peers)

    fx_part = fx_v.at[pl.ds(0, N - 1), 0]
    bytes_of(fx_part, fx_sem.at[1])
    swap = pltpu.make_async_remote_copy(
        src_ref=fx_v.at[:, core], dst_ref=fx_v.at[:, core], send_sem=fx_sem.at[2], recv_sem=fx_sem.at[3],
        device_id={"gy": gy + 1 - 2 * core}, device_id_type=MESH,
    )
    swap.start()
    swap.wait()
    fx = fx_v[...].reshape(ROWS, ROWS)
    fx_parts[0], fx_parts[1] = split(fx)
    fxt_parts[0], fxt_parts[1] = split(jnp.transpose(fx))

    arrived(X_IN)
    t_v[...] = dot((fx_parts[0], fx_parts[1]), split(recv_v[X_IN]))
    bytes_of(exp_recv.at[pl.ds(0, (N - 1) * 16)], exp_sem.at[1])
    arrived(SUMS)

    for begin in range(0, 256, GROUP):
        firsts, seconds = [], []
        for k in range(begin // 16, (begin + GROUP) // 16):
            first, second = pack(t_v[k * 32 : k * 32 + 16, :], t_v[k * 32 + 16 : k * 32 + 32, :])
            firsts.append(first)
            seconds.append(second)
        f0 = jnp.concatenate(firsts, axis=0) * LOG2E
        f1 = jnp.concatenate(seconds, axis=0) * LOG2E

        def mark(m, total):
            l0 = load_ref[0, m]
            l1 = load_ref[1, m]
            rate = jnp.exp2(l0 * f0 + (l1 * f1 + (off_ref[m] * LOG2E - SHIFT)))
            return total[0] + l0 * rate, total[1] + l1 * rate

        zero = jnp.zeros((GROUP, 128), F32)
        a0, a1 = lax.fori_loop(0, MARKS, mark, (zero, zero), unroll=4)
        scale = exp_recv[begin : begin + GROUP, :] * (2.0**SHIFT)
        upper, lower = pack(scale * a0, scale * a1)
        for n in range(GROUP // 16):
            k = begin // 16 + n
            t_v[k * 32 : k * 32 + 16, :] = recv_v[SUMS, k * 32 : k * 32 + 16, :] - upper[n * 16 : n * 16 + 16]
            t_v[k * 32 + 16 : k * 32 + 32, :] = recv_v[SUMS, k * 32 + 16 : k * 32 + 32, :] - lower[n * 16 : n * 16 + 16]

    back = dot(split(t_v[...]), time)
    send_v[X_OUT] = dot((fxt_parts[0], fxt_parts[1]), split(back))
    exchange(X_OUT, gx, x_peers)
    arrived(X_OUT)
    lines_to_columns(lambda rows: recv_v[X_OUT, rows, :], BY_IN)
    exchange(BY_IN, j, y_peers)
    arrived(BY_IN)
    y_mix(BY_IN, BY_OUT, (fyt_parts[0], fyt_parts[1]))
    exchange(BY_OUT, j, y_peers)
    arrived(BY_OUT)
    for g in range(8):
        cols = slice(g * 128, g * 128 + 128)
        first, second = pack(
            recv_v[BY_OUT, pl.ds(2 * g, 32, stride=16), :], recv_v[BY_OUT, pl.ds(2 * g + 1, 32, stride=16), :]
        )
        out_ref[0, :, cols] = first - w_v[0, :, cols]
        out_ref[1, :, cols] = second - w_v[1, :, cols]

    for phase in range(7):
        sent(phase)
    bytes_of(exp_send.at[pl.ds(0, (N - 1) * 16)], exp_sem.at[0])
    bytes_of(fy_part, fy_sem.at[0])
    bytes_of(fx_part, fx_sem.at[0])


def body(whitened, factor_x, factor_y, factor_t, mark_loadings, mark_offsets, exposure, counts):
    fx = factor_x.reshape(2, 16, 512)
    return pl.pallas_call(
        kernel,
        out_shape=jax.ShapeDtypeStruct((2, 32, 1024), F32),
        in_specs=[pl.BlockSpec(memory_space=pltpu.HBM)] * 8,
        out_specs=pl.BlockSpec(memory_space=pltpu.VMEM),
        scratch_shapes=[
            pltpu.SMEM((2, MARKS), F32),
            pltpu.SMEM((MARKS,), F32),
            pltpu.VMEM((2, 32, 1024), F32),
            pltpu.VMEM((32, 1024), F32),
            pltpu.VMEM((MARKS, 32, 1024), jnp.int32),
            pltpu.VMEM((2, 32, 1024), F32),
            pltpu.VMEM((64, 64), F32),
            pltpu.VMEM((N, 2, 16, 512), F32),
            pltpu.VMEM((2, 512, 512), BF16),
            pltpu.VMEM((2, 512, 512), BF16),
            pltpu.VMEM((N, 16, 256), F32),
            pltpu.VMEM((2, 256, 256), BF16),
            pltpu.VMEM((ROWS, 128), F32),
            pltpu.VMEM((7, ROWS, 128), F32),
            pltpu.VMEM((7, ROWS, 128), F32),
            pltpu.VMEM((256, 128), F32),
            pltpu.VMEM((256, 128), F32),
            pltpu.SemaphoreType.DMA((8,)),
            pltpu.SemaphoreType.DMA((7,)),
            pltpu.SemaphoreType.DMA((7,)),
            pltpu.SemaphoreType.DMA((2,)),
            pltpu.SemaphoreType.DMA((4,)),
            pltpu.SemaphoreType.DMA((2,)),
        ],
        compiler_params=pltpu.CompilerParams(
            collective_id=0, has_side_effects=True, vmem_limit_bytes=60 * 1024 * 1024
        ),
    )(mark_loadings, mark_offsets, whitened, fx, factor_y, factor_t, exposure, counts)


def solution(mesh):
    placed = (
        P(None, "gx", ("gy", "ta")),
        P("gx", None),
        P(("gy", "ta"), None),
        P(),
        P(),
        P(),
        P("gx", ("gy", "ta")),
        P(None, "gx", ("gy", "ta")),
    )
    return jax.shard_map(
        body, mesh=mesh, in_specs=placed, out_specs=P(None, "gx", ("gy", "ta")), check_vma=False
    )
```

profile of v0, /device:TPU:1, one launch (start us, length us, event | category | flops | bytes accessed | tf_op | source)
XLA Modules:
  0.0 67.2 jit_solution(17731036285688614249)
XLA Ops:
  0.0 65.5 %shard_map.82 = f32[2,32,1024]{2,1,0:T(8,128)} custom-call(f32[2,64]{1,0:T(2,128)} %load_hbm.1, f32[64]{0:T(128)} %off_hbm.1, f32[2,32,1024]{2,1,0:T(8,128)} %w_hbm.1, f32[2,16,512]{2,1,0:T(8,128)} %bitcast.1, f32[16,256]{1,0:T(8,128)} %fy_hbm.1, f32[64,64]{1,0:T(8,128)} %ft_hbm.1, f32[32,1024]{1,0:T(8,128)} %exp_hbm.1, s32[64,32,1024]{2,1,0:T(8,128)} %counts_hbm.1), custom_call_target="tpu_custom_call" | custom-call | tf_op jit(solution)/shard_map/pallas_call | solution.py:268
  65.5 1.7 %copy.10 = f32[2,32,1024]{2,1,0:T(8,128)} copy(f32[2,32,1024]{2,1,0:T(8,128)} %shard_map.82) | data formatting | bytes 524288
where the time goes:
time: 67.3 us; the launch traced here: 67.2 us
  Pallas kernels  65.5 us (97%)
  local copies, waits for them, and re-layouts  1.67 us (2%)
    pallas_call x1, Pallas kernels, body(): pl.pallas_call(kernel, out_shape=jax.ShapeDtypeStruct((2, 32, 1024), F32)...  65.5 us
    unnamed x1, local copies, waits for them, and re-layouts  1.67 us

commit v1 on v0

--- a/solution.py
+++ b/solution.py
@@ -55,6 +55,7 @@
     ta = lax.axis_index("ta")
     j = gy * 2 + ta
     core = lax.rem(gy, 2)
+    row = gy // 2
 
     def x_peer(step):
         x = gx // 8
@@ -75,8 +76,11 @@
         (
             (w_hbm, w_v),
             (ft_hbm, ft_v),
-            (fy_hbm, fy_v.at[j]),
-            (fx_hbm.at[core], fx_v.at[gx, core]),
+            (fy_hbm, fy_v.at[row, core, ta]),
+            (
+                fx_hbm.at[pl.ds(pl.multiple_of(row * 8, 8), 8), pl.ds(pl.multiple_of(core * 256, 256), 256)],
+                fx_v.at[core, gx, row],
+            ),
             (load_hbm, load_ref),
             (off_hbm, off_ref),
             (exp_hbm, exp_v),
@@ -163,11 +167,13 @@
 
     pl.semaphore_wait(barrier, 2 * (N - 1))
 
-    for _, at in y_peers:
-        push(fy_v.at[j], fy_v.at[j], fy_sem.at[0], fy_sem.at[1], at)
+    mine = fy_v.at[row, core, ta]
+    for step, (_, at) in zip(Y_STEPS, y_peers):
+        if step[1] == 0:
+            push(mine, mine, fy_sem.at[0], fy_sem.at[1], at)
     exchange(Y_IN, j, y_peers)
     for _, at in x_peers:
-        push(fx_v.at[gx, core], fx_v.at[gx, core], fx_sem.at[0], fx_sem.at[1], at)
+        push(fx_v.at[core, gx, row], fx_v.at[core, gx, row], fx_sem.at[0], fx_sem.at[1], at)
 
     for number in range(4, 8):
         loads[number].wait()
@@ -184,12 +190,22 @@
     send_v[SUMS] = lines(sums_v)
     exchange(SUMS, gx, x_peers)
 
-    fy_part = fy_v.at[pl.ds(0, N - 1)]
+    other = {"gy": gy + 1 - 2 * core}
+    fy_half = fy_v.at[:, core]
+    fy_part = recv_v.at[Y_IN, pl.ds(0, 7 * PIECE)]
     bytes_of(fy_part, fy_sem.at[1])
+    push(fy_half, fy_half, fy_sem.at[2], fy_sem.at[3], other)
+    arrived(Y_IN)
+    bytes_of(fy_half, fy_sem.at[3])
     fy = fy_v[...].reshape(256, 256)
-    arrived(Y_IN)
     y_mix(Y_IN, Y_OUT, split(fy))
     exchange(Y_OUT, j, y_peers)
+
+    fx_eighth = fx_v.at[0, pl.ds(0, N - 1), 0]
+    bytes_of(fx_eighth, fx_sem.at[1])
+    for step in (2, 1, 3):
+        at = {"gy": lax.rem(row + step, 4) * 2 + core}
+        push(fx_v.at[core, :, row], fx_v.at[core, :, row], fx_sem.at[2], fx_sem.at[3], at)
     fyt_parts[0], fyt_parts[1] = split(jnp.transpose(fy))
     arrived(Y_OUT)
 
@@ -197,15 +213,11 @@
         send_v[X_IN, pl.ds(y * 32, 32), :] = recv_v[Y_OUT, pl.ds(y, 32, stride=16), :]
     exchange(X_IN, gx, x_peers)
 
-    fx_part = fx_v.at[pl.ds(0, N - 1), 0]
-    bytes_of(fx_part, fx_sem.at[1])
-    swap = pltpu.make_async_remote_copy(
-        src_ref=fx_v.at[:, core], dst_ref=fx_v.at[:, core], send_sem=fx_sem.at[2], recv_sem=fx_sem.at[3],
-        device_id={"gy": gy + 1 - 2 * core}, device_id_type=MESH,
-    )
-    swap.start()
-    swap.wait()
-    fx = fx_v[...].reshape(ROWS, ROWS)
+    fx_half = fx_v.at[0, :, pl.ds(0, 3)]
+    bytes_of(fx_half, fx_sem.at[3])
+    push(fx_v.at[core], fx_v.at[core], fx_sem.at[4], fx_sem.at[5], other)
+    bytes_of(fx_v.at[0], fx_sem.at[5])
+    fx = jnp.concatenate([fx_v[0].reshape(ROWS, 256), fx_v[1].reshape(ROWS, 256)], axis=1)
     fx_parts[0], fx_parts[1] = split(fx)
     fxt_parts[0], fxt_parts[1] = split(jnp.transpose(fx))
 
@@ -253,19 +265,21 @@
         first, second = pack(
             recv_v[BY_OUT, pl.ds(2 * g, 32, stride=16), :], recv_v[BY_OUT, pl.ds(2 * g + 1, 32, stride=16), :]
         )
-        out_ref[0, :, cols] = first - w_v[0, :, cols]
-        out_ref[1, :, cols] = second - w_v[1, :, cols]
+        out_ref[0, :, cols] = first
+        out_ref[1, :, cols] = second
 
     for phase in range(7):
         sent(phase)
     bytes_of(exp_send.at[pl.ds(0, (N - 1) * 16)], exp_sem.at[0])
     bytes_of(fy_part, fy_sem.at[0])
-    bytes_of(fx_part, fx_sem.at[0])
+    bytes_of(fy_half, fy_sem.at[2])
+    bytes_of(fx_eighth, fx_sem.at[0])
+    bytes_of(fx_half, fx_sem.at[2])
+    bytes_of(fx_v.at[0], fx_sem.at[4])
 
 
 def body(whitened, factor_x, factor_y, factor_t, mark_loadings, mark_offsets, exposure, counts):
-    fx = factor_x.reshape(2, 16, 512)
-    return pl.pallas_call(
+    back = pl.pallas_call(
         kernel,
         out_shape=jax.ShapeDtypeStruct((2, 32, 1024), F32),
         in_specs=[pl.BlockSpec(memory_space=pltpu.HBM)] * 8,
@@ -278,10 +292,10 @@
             pltpu.VMEM((MARKS, 32, 1024), jnp.int32),
             pltpu.VMEM((2, 32, 1024), F32),
             pltpu.VMEM((64, 64), F32),
-            pltpu.VMEM((N, 2, 16, 512), F32),
+            pltpu.VMEM((2, N, 4, 8, 256), F32),
             pltpu.VMEM((2, 512, 512), BF16),
             pltpu.VMEM((2, 512, 512), BF16),
-            pltpu.VMEM((N, 16, 256), F32),
+            pltpu.VMEM((4, 2, 2, 16, 256), F32),
             pltpu.VMEM((2, 256, 256), BF16),
             pltpu.VMEM((ROWS, 128), F32),
             pltpu.VMEM((7, ROWS, 128), F32),
@@ -292,13 +306,14 @@
             pltpu.SemaphoreType.DMA((7,)),
             pltpu.SemaphoreType.DMA((7,)),
             pltpu.SemaphoreType.DMA((2,)),
+            pltpu.SemaphoreType.DMA((6,)),
             pltpu.SemaphoreType.DMA((4,)),
-            pltpu.SemaphoreType.DMA((2,)),
         ],
         compiler_params=pltpu.CompilerParams(
             collective_id=0, has_side_effects=True, vmem_limit_bytes=60 * 1024 * 1024
         ),
-    )(mark_loadings, mark_offsets, whitened, fx, factor_y, factor_t, exposure, counts)
+    )(mark_loadings, mark_offsets, whitened, factor_x, factor_y, factor_t, exposure, counts)
+    return back - whitened
 
 
 def solution(mesh):

time: 67.3 us -> 64.3 us (0.955)
  Pallas kernels: 65.5 us -> 62.5 us
  other arithmetic: 0 us -> 1.68 us
  local copies, waits for them, and re-layouts: 1.67 us -> 0.01 us
    pallas_call x1, Pallas kernels: 65.5 us -> 62.5 us  [body(): pl.pallas_call(kernel, out_shape=jax.ShapeDtypeStruct((2, 32, 1024), F32)...]
    sub x0 -> x1, other arithmetic: none -> 1.68 us  [body(): return back - whitened]
    unnamed x1 -> x2, local copies, waits for them, and re-layouts: 1.67 us -> 0.01 us
where the time goes in v1:
time: 64.3 us; the launch traced here: 64.2 us
  Pallas kernels  62.5 us (97%)
  other arithmetic  1.68 us (3%)
    pallas_call x1, Pallas kernels, body(): pl.pallas_call(kernel, out_shape=jax.ShapeDtypeStruct((2, 32, 1024), F32)...  62.5 us
    sub x1, other arithmetic, body(): return back - whitened  1.68 us

profile of v1, /device:TPU:1, one launch (start us, length us, event | category | flops | bytes accessed | tf_op | source)
XLA Modules:
  0.0 64.2 jit_solution(13936905001939366718)
XLA Ops:
  0.0 0.0 copy-start
  0.0 62.5 %shard_map.82 = f32[2,32,1024]{2,1,0:T(8,128)} custom-call(f32[2,64]{1,0:T(2,128)} %load_hbm.1, f32[64]{0:T(128)} %off_hbm.1, f32[2,32,1024]{2,1,0:T(8,128)} %w_hbm.1, f32[32,512]{1,0:T(8,128)} %fx_hbm.1, f32[16,256]{1,0:T(8,128)} %fy_hbm.1, f32[64,64]{1,0:T(8,128)} %ft_hbm.1, f32[32,1024]{1,0:T(8,128)} %exp_hbm.1, s32[64,32,1024]{2,1,0:T(8,128)} %counts_hbm.1), custom_call_target="tpu_custom_call" | custom-call | tf_op jit(solution)/shard_map/pallas_call | solution.py:282
  62.5 0.0 copy-done
  62.5 1.7 %sub.3 = f32[2,32,1024]{2,1,0:T(8,128)} subtract(f32[2,32,1024]{2,1,0:T(8,128)} %shard_map.82, f32[2,32,1024]{2,1,0:T(8,128)S(1)} %copy-done) | non-fusion elementwise | flops 65536 | bytes 786432 | tf_op jit(solution)/shard_map/sub | solution.py:316
Async XLA Ops:
  0.0 62.5 %copy-start = (f32[2,32,1024]{2,1,0:T(8,128)S(1)}, f32[2,32,1024]{2,1,0:T(8,128)}, u32[]{:S(2)}) copy-start(f32[2,32,1024]{2,1,0:T(8,128)} %w_hbm.1) | copy-start | bytes 786436

commit v2 on v1

--- a/solution.py
+++ b/solution.py
@@ -12,8 +12,9 @@
 BF16 = jnp.bfloat16
 LOG2E = math.log2(math.e)
 N = 16
-PIECE = 32
-ROWS = N * PIECE
+PIECE = 16
+HALF = N * PIECE
+ROWS = 2 * HALF
 MARKS = 64
 SHIFT = 8.0
 GROUP = 64
@@ -39,6 +40,11 @@
     return one(a[0], b[0]) + (one(a[0], b[1]) + one(a[1], b[0]))
 
 
+def dot_wide(a, b):
+    both = jnp.dot(a[0], jnp.concatenate([b[0], b[1]], axis=1), preferred_element_type=F32)
+    return both[:, :128] + (both[:, 128:] + jnp.dot(a[1], b[0], preferred_element_type=F32))
+
+
 def swap_halves(a):
     return pltpu.roll(a, 64, 1)
 
@@ -47,8 +53,8 @@
     load_hbm, off_hbm, w_hbm, fx_hbm, fy_hbm, ft_hbm, exp_hbm, counts_hbm, out_ref,
     load_ref, off_ref, w_v, exp_v, counts_v, sums_v, ft_v,
     fx_v, fx_parts, fxt_parts, fy_v, fyt_parts,
-    t_v, send_v, recv_v, exp_send, exp_recv,
-    local_sem, send_sem, recv_sem, exp_sem, fx_sem, fy_sem,
+    t_v, field_v, send_v, recv_v, exp_send, exp_recv,
+    local_sem, send_sem, recv_sem, sums_sem, exp_sem, fx_sem, fy_sem,
 ):
     gx = lax.axis_index("gx")
     gy = lax.axis_index("gy")
@@ -99,22 +105,29 @@
             src_ref=source, dst_ref=target, send_sem=sends, recv_sem=receives, device_id=at, device_id_type=MESH
         ).start()
 
-    def rows_of(k, piece=PIECE):
-        return pl.ds(pl.multiple_of(k * piece, piece), piece)
-
-    def exchange(phase, me, peers):
+    def rows_of(k, piece, base=0):
+        return pl.ds(pl.multiple_of(base + k * piece, piece), piece)
+
+    def exchange(phase, half, me, peers):
+        mine = rows_of(me, PIECE, half * HALF)
         for k, at in peers:
-            push(send_v.at[phase, rows_of(k)], recv_v.at[phase, rows_of(me)], send_sem.at[phase], recv_sem.at[phase], at)
-        recv_v[phase, rows_of(me), :] = send_v[phase, rows_of(me), :]
+            push(
+                send_v.at[phase, rows_of(k, PIECE, half * HALF)],
+                recv_v.at[phase, mine],
+                send_sem.at[phase, half],
+                recv_sem.at[phase, half],
+                at,
+            )
+        recv_v[phase, mine, :] = send_v[phase, mine, :]
 
     def bytes_of(part, sem):
         pltpu.make_async_copy(part, part, sem).wait()
 
-    def arrived(phase):
-        bytes_of(recv_v.at[phase, pl.ds(0, ROWS - PIECE)], recv_sem.at[phase])
-
-    def sent(phase):
-        bytes_of(send_v.at[phase, pl.ds(0, ROWS - PIECE)], send_sem.at[phase])
+    def arrived(phase, half):
+        bytes_of(recv_v.at[phase, pl.ds(0, HALF - PIECE)], recv_sem.at[phase, half])
+
+    def sent(phase, half):
+        bytes_of(send_v.at[phase, pl.ds(0, HALF - PIECE)], send_sem.at[phase, half])
 
     def low(rows):
         return lax.broadcasted_iota(jnp.int32, (rows, 128), 1) < 64
@@ -129,19 +142,13 @@
             found += pack(ref[0, :, g * 128 : g * 128 + 128], ref[1, :, g * 128 : g * 128 + 128])
         return jnp.concatenate(found, axis=0)
 
-    def lines_to_columns(load, phase):
-        for x in range(32):
-            send_v[phase, pl.ds(x * 16, 16), :] = load(pl.ds(x, 16, stride=32))
-
-    def y_mix(source, target, matrix):
-        both = [
-            jnp.concatenate([recv_v[source, pl.ds(k * PIECE + h * 16, 16), :] for k in range(N)], axis=0)
-            for h in range(2)
-        ]
-        mixed = dot(matrix, split(jnp.concatenate(both, axis=1)))
-        for k in range(N):
-            for h in range(2):
-                send_v[target, pl.ds(k * PIECE + h * 16, 16), :] = mixed[k * 16 : k * 16 + 16, h * 128 : h * 128 + 128]
+    def turn(load, phase, half):
+        for n in range(N):
+            send_v[phase, pl.ds(half * HALF + n * N, N), :] = load(n)
+
+    def y_mix(source, target, half, matrix):
+        rows = pl.ds(half * HALF, HALF)
+        send_v[target, rows, :] = dot_wide(matrix, split(recv_v[source, rows, :]))
 
     def sum_counts():
         for xt in range(4):
@@ -163,7 +170,8 @@
         )
     )
     t_v[...] = dot(split(lines(w_v)), time, ((1,), (1,)))
-    lines_to_columns(lambda rows: t_v[rows, :], Y_IN)
+    for half in range(2):
+        turn(lambda n: t_v[pl.ds(half * N + n, N, stride=32), :], Y_IN, half)
 
     pl.semaphore_wait(barrier, 2 * (N - 1))
 
@@ -171,7 +179,8 @@
     for step, (_, at) in zip(Y_STEPS, y_peers):
         if step[1] == 0:
             push(mine, mine, fy_sem.at[0], fy_sem.at[1], at)
-    exchange(Y_IN, j, y_peers)
+    for half in range(2):
+        exchange(Y_IN, half, j, y_peers)
     for _, at in x_peers:
         push(fx_v.at[core, gx, row], fx_v.at[core, gx, row], fx_sem.at[0], fx_sem.at[1], at)
 
@@ -183,23 +192,27 @@
         exp_send[g * 32 : g * 32 + 16, :] = even
         exp_send[g * 32 + 16 : g * 32 + 32, :] = odd
     for k, at in x_peers:
-        push(exp_send.at[rows_of(k, 16)], exp_recv.at[rows_of(gx, 16)], exp_sem.at[0], exp_sem.at[1], at)
-    exp_recv[rows_of(gx, 16), :] = exp_send[rows_of(gx, 16), :]
+        push(exp_send.at[rows_of(k, PIECE)], exp_recv.at[rows_of(gx, PIECE)], exp_sem.at[0], exp_sem.at[1], at)
+    exp_recv[rows_of(gx, PIECE), :] = exp_send[rows_of(gx, PIECE), :]
 
     sum_counts()
     send_v[SUMS] = lines(sums_v)
-    exchange(SUMS, gx, x_peers)
+    for k, at in x_peers:
+        push(send_v.at[SUMS, rows_of(k, 32)], recv_v.at[SUMS, rows_of(gx, 32)], sums_sem.at[0], sums_sem.at[1], at)
+    recv_v[SUMS, rows_of(gx, 32), :] = send_v[SUMS, rows_of(gx, 32), :]
 
     other = {"gy": gy + 1 - 2 * core}
     fy_half = fy_v.at[:, core]
-    fy_part = recv_v.at[Y_IN, pl.ds(0, 7 * PIECE)]
+    fy_part = recv_v.at[Y_IN, pl.ds(0, 7 * 32)]
     bytes_of(fy_part, fy_sem.at[1])
     push(fy_half, fy_half, fy_sem.at[2], fy_sem.at[3], other)
-    arrived(Y_IN)
     bytes_of(fy_half, fy_sem.at[3])
     fy = fy_v[...].reshape(256, 256)
-    y_mix(Y_IN, Y_OUT, split(fy))
-    exchange(Y_OUT, j, y_peers)
+    fy_parts = split(fy)
+    for half in range(2):
+        arrived(Y_IN, half)
+        y_mix(Y_IN, Y_OUT, half, fy_parts)
+        exchange(Y_OUT, half, j, y_peers)
 
     fx_eighth = fx_v.at[0, pl.ds(0, N - 1), 0]
     bytes_of(fx_eighth, fx_sem.at[1])
@@ -207,11 +220,10 @@
         at = {"gy": lax.rem(row + step, 4) * 2 + core}
         push(fx_v.at[core, :, row], fx_v.at[core, :, row], fx_sem.at[2], fx_sem.at[3], at)
     fyt_parts[0], fyt_parts[1] = split(jnp.transpose(fy))
-    arrived(Y_OUT)
-
-    for y in range(N):
-        send_v[X_IN, pl.ds(y * 32, 32), :] = recv_v[Y_OUT, pl.ds(y, 32, stride=16), :]
-    exchange(X_IN, gx, x_peers)
+    for half in range(2):
+        arrived(Y_OUT, half)
+        turn(lambda n: recv_v[Y_OUT, pl.ds(half * HALF + n, N, stride=N), :], X_IN, half)
+        exchange(X_IN, half, gx, x_peers)
 
     fx_half = fx_v.at[0, :, pl.ds(0, 3)]
     bytes_of(fx_half, fx_sem.at[3])
@@ -219,21 +231,31 @@
     bytes_of(fx_v.at[0], fx_sem.at[5])
     fx = jnp.concatenate([fx_v[0].reshape(ROWS, 256), fx_v[1].reshape(ROWS, 256)], axis=1)
     fx_parts[0], fx_parts[1] = split(fx)
-    fxt_parts[0], fxt_parts[1] = split(jnp.transpose(fx))
-
-    arrived(X_IN)
-    t_v[...] = dot((fx_parts[0], fx_parts[1]), split(recv_v[X_IN]))
+    turned = split(jnp.transpose(fx))
+    for part in range(2):
+        for half in range(2):
+            for k in range(N):
+                x = k * 32 + half * 16
+                fxt_parts[part, half, k * 16 : k * 16 + 16, :] = turned[part][x : x + 16, :]
+
+    for half in range(2):
+        arrived(X_IN, half)
+    gathered = jnp.concatenate(
+        [recv_v[X_IN, pl.ds(half * HALF + k * PIECE, PIECE), :] for k in range(N) for half in range(2)], axis=0
+    )
+    field = dot_wide((fx_parts[0], fx_parts[1]), split(gathered)) * LOG2E
+    for k in range(N):
+        first, second = pack(field[k * 32 : k * 32 + 16], field[k * 32 + 16 : k * 32 + 32])
+        field_v[0, k * 16 : k * 16 + 16, :] = first
+        field_v[1, k * 16 : k * 16 + 16, :] = second
+    sums_part = recv_v.at[SUMS, pl.ds(0, ROWS - 32)]
     bytes_of(exp_recv.at[pl.ds(0, (N - 1) * 16)], exp_sem.at[1])
-    arrived(SUMS)
-
-    for begin in range(0, 256, GROUP):
-        firsts, seconds = [], []
-        for k in range(begin // 16, (begin + GROUP) // 16):
-            first, second = pack(t_v[k * 32 : k * 32 + 16, :], t_v[k * 32 + 16 : k * 32 + 32, :])
-            firsts.append(first)
-            seconds.append(second)
-        f0 = jnp.concatenate(firsts, axis=0) * LOG2E
-        f1 = jnp.concatenate(seconds, axis=0) * LOG2E
+    bytes_of(sums_part, sums_sem.at[1])
+
+    for begin in range(0, HALF, GROUP):
+        rows = slice(begin, begin + GROUP)
+        f0 = field_v[0, rows, :]
+        f1 = field_v[1, rows, :]
 
         def mark(m, total):
             l0 = load_ref[0, m]
@@ -242,34 +264,39 @@
             return total[0] + l0 * rate, total[1] + l1 * rate
 
         zero = jnp.zeros((GROUP, 128), F32)
-        a0, a1 = lax.fori_loop(0, MARKS, mark, (zero, zero), unroll=4)
-        scale = exp_recv[begin : begin + GROUP, :] * (2.0**SHIFT)
-        upper, lower = pack(scale * a0, scale * a1)
-        for n in range(GROUP // 16):
-            k = begin // 16 + n
-            t_v[k * 32 : k * 32 + 16, :] = recv_v[SUMS, k * 32 : k * 32 + 16, :] - upper[n * 16 : n * 16 + 16]
-            t_v[k * 32 + 16 : k * 32 + 32, :] = recv_v[SUMS, k * 32 + 16 : k * 32 + 32, :] - lower[n * 16 : n * 16 + 16]
-
-    back = dot(split(t_v[...]), time)
-    send_v[X_OUT] = dot((fxt_parts[0], fxt_parts[1]), split(back))
-    exchange(X_OUT, gx, x_peers)
-    arrived(X_OUT)
-    lines_to_columns(lambda rows: recv_v[X_OUT, rows, :], BY_IN)
-    exchange(BY_IN, j, y_peers)
-    arrived(BY_IN)
-    y_mix(BY_IN, BY_OUT, (fyt_parts[0], fyt_parts[1]))
-    exchange(BY_OUT, j, y_peers)
-    arrived(BY_OUT)
-    for g in range(8):
-        cols = slice(g * 128, g * 128 + 128)
-        first, second = pack(
-            recv_v[BY_OUT, pl.ds(2 * g, 32, stride=16), :], recv_v[BY_OUT, pl.ds(2 * g + 1, 32, stride=16), :]
-        )
-        out_ref[0, :, cols] = first
-        out_ref[1, :, cols] = second
-
-    for phase in range(7):
-        sent(phase)
+        field_v[0, rows, :], field_v[1, rows, :] = lax.fori_loop(0, MARKS, mark, (zero, zero), unroll=16)
+
+    residual = []
+    for k in range(N):
+        rows = slice(k * 16, k * 16 + 16)
+        scale = exp_recv[rows, :] * (2.0**SHIFT)
+        residual += pack(scale * field_v[0, rows, :], scale * field_v[1, rows, :])
+    back = split(dot(split(recv_v[SUMS] - jnp.concatenate(residual, axis=0)), time))
+    for half in range(2):
+        send_v[X_OUT, pl.ds(half * HALF, HALF), :] = dot_wide((fxt_parts[0, half], fxt_parts[1, half]), back)
+        exchange(X_OUT, half, gx, x_peers)
+    for half in range(2):
+        arrived(X_OUT, half)
+        turn(lambda n: recv_v[X_OUT, pl.ds(half * HALF + n, N, stride=N), :], BY_IN, half)
+        exchange(BY_IN, half, j, y_peers)
+    for half in range(2):
+        arrived(BY_IN, half)
+        y_mix(BY_IN, BY_OUT, half, (fyt_parts[0], fyt_parts[1]))
+        exchange(BY_OUT, half, j, y_peers)
+    for half in range(2):
+        arrived(BY_OUT, half)
+        xs = slice(half * 16, half * 16 + 16)
+        for g in range(8):
+            cols = slice(g * 128, g * 128 + 128)
+            out_ref[0, xs, cols], out_ref[1, xs, cols] = pack(
+                recv_v[BY_OUT, pl.ds(half * HALF + 2 * g, N, stride=N), :],
+                recv_v[BY_OUT, pl.ds(half * HALF + 2 * g + 1, N, stride=N), :],
+            )
+
+    for phase in range(6):
+        for half in range(2):
+            sent(phase, half)
+    bytes_of(sums_part, sums_sem.at[0])
     bytes_of(exp_send.at[pl.ds(0, (N - 1) * 16)], exp_sem.at[0])
     bytes_of(fy_part, fy_sem.at[0])
     bytes_of(fy_half, fy_sem.at[2])
@@ -294,17 +321,19 @@
             pltpu.VMEM((64, 64), F32),
             pltpu.VMEM((2, N, 4, 8, 256), F32),
             pltpu.VMEM((2, 512, 512), BF16),
-            pltpu.VMEM((2, 512, 512), BF16),
+            pltpu.VMEM((2, 2, HALF, 512), BF16),
             pltpu.VMEM((4, 2, 2, 16, 256), F32),
             pltpu.VMEM((2, 256, 256), BF16),
             pltpu.VMEM((ROWS, 128), F32),
+            pltpu.VMEM((2, HALF, 128), F32),
             pltpu.VMEM((7, ROWS, 128), F32),
             pltpu.VMEM((7, ROWS, 128), F32),
             pltpu.VMEM((256, 128), F32),
             pltpu.VMEM((256, 128), F32),
             pltpu.SemaphoreType.DMA((8,)),
-            pltpu.SemaphoreType.DMA((7,)),
-            pltpu.SemaphoreType.DMA((7,)),
+            pltpu.SemaphoreType.DMA((6, 2)),
+            pltpu.SemaphoreType.DMA((6, 2)),
+            pltpu.SemaphoreType.DMA((2,)),
             pltpu.SemaphoreType.DMA((2,)),
             pltpu.SemaphoreType.DMA((6,)),
             pltpu.SemaphoreType.DMA((4,)),

time: 64.3 us -> 59 us (0.918)
  Pallas kernels: 62.5 us -> 57.2 us
    pallas_call x1, Pallas kernels: 62.5 us -> 57.2 us  [body(): pl.pallas_call(kernel, out_shape=jax.ShapeDtypeStruct((2, 32, 1024), F32)...]
where the time goes in v2:
time: 59 us; the launch traced here: 58.9 us
  Pallas kernels  57.2 us (97%)
  other arithmetic  1.68 us (3%)
    pallas_call x1, Pallas kernels, body(): pl.pallas_call(kernel, out_shape=jax.ShapeDtypeStruct((2, 32, 1024), F32)...  57.2 us
    sub x1, other arithmetic, body(): return back - whitened  1.68 us

profile of v2, /device:TPU:1, one launch (start us, length us, event | category | flops | bytes accessed | tf_op | source)
XLA Modules:
  0.0 58.9 jit_solution(10442047231720367882)
XLA Ops:
  0.0 0.0 copy-start
  0.0 57.2 %shard_map.82 = f32[2,32,1024]{2,1,0:T(8,128)} custom-call(f32[2,64]{1,0:T(2,128)} %load_hbm.1, f32[64]{0:T(128)} %off_hbm.1, f32[2,32,1024]{2,1,0:T(8,128)} %w_hbm.1, f32[32,512]{1,0:T(8,128)} %fx_hbm.1, f32[16,256]{1,0:T(8,128)} %fy_hbm.1, f32[64,64]{1,0:T(8,128)} %ft_hbm.1, f32[32,1024]{1,0:T(8,128)} %exp_hbm.1, s32[64,32,1024]{2,1,0:T(8,128)} %counts_hbm.1), custom_call_target="tpu_custom_call" | custom-call | tf_op jit(solution)/shard_map/pallas_call | solution.py:309
  57.2 0.0 copy-done
  57.2 1.7 %sub.3 = f32[2,32,1024]{2,1,0:T(8,128)} subtract(f32[2,32,1024]{2,1,0:T(8,128)} %shard_map.82, f32[2,32,1024]{2,1,0:T(8,128)S(1)} %copy-done) | non-fusion elementwise | flops 65536 | bytes 786432 | tf_op jit(solution)/shard_map/sub | solution.py:345
Async XLA Ops:
  0.0 57.2 %copy-start = (f32[2,32,1024]{2,1,0:T(8,128)S(1)}, f32[2,32,1024]{2,1,0:T(8,128)}, u32[]{:S(2)}) copy-start(f32[2,32,1024]{2,1,0:T(8,128)} %w_hbm.1) | copy-start | bytes 786436

commit v3 on v2

--- a/solution.py
+++ b/solution.py
@@ -51,7 +51,7 @@
 
 def kernel(
     load_hbm, off_hbm, w_hbm, fx_hbm, fy_hbm, ft_hbm, exp_hbm, counts_hbm, out_ref,
-    load_ref, off_ref, w_v, exp_v, counts_v, sums_v, ft_v,
+    load_ref, off_ref, rate_off, w_v, exp_v, counts_v, sums_v, ft_v,
     fx_v, fx_parts, fxt_parts, fy_v, fyt_parts,
     t_v, field_v, send_v, recv_v, exp_send, exp_recv,
     local_sem, send_sem, recv_sem, sums_sem, exp_sem, fx_sem, fy_sem,
@@ -76,6 +76,10 @@
 
     x_peers = [x_peer(step) for step in X_STEPS]
     y_peers = [y_peer(step) for step in Y_STEPS]
+
+    barrier = pltpu.get_barrier_semaphore()
+    for _, at in x_peers + y_peers:
+        pl.semaphore_signal(barrier, inc=1, device_id=at, device_id_type=MESH)
 
     loads = []
     for number, (source, target) in enumerate(
@@ -96,10 +100,6 @@
         loads.append(pltpu.make_async_copy(source, target, local_sem.at[number]))
         loads[-1].start()
 
-    barrier = pltpu.get_barrier_semaphore()
-    for _, at in y_peers + x_peers:
-        pl.semaphore_signal(barrier, inc=1, device_id=at, device_id_type=MESH)
-
     def push(source, target, sends, receives, at):
         pltpu.make_async_remote_copy(
             src_ref=source, dst_ref=target, send_sem=sends, recv_sem=receives, device_id=at, device_id_type=MESH
@@ -181,9 +181,6 @@
             push(mine, mine, fy_sem.at[0], fy_sem.at[1], at)
     for half in range(2):
         exchange(Y_IN, half, j, y_peers)
-    for _, at in x_peers:
-        push(fx_v.at[core, gx, row], fx_v.at[core, gx, row], fx_sem.at[0], fx_sem.at[1], at)
-
     for number in range(4, 8):
         loads[number].wait()
     for g in range(8):
@@ -191,16 +188,20 @@
         even, odd = pack(exp_v[0:16, cols], exp_v[16:32, cols])
         exp_send[g * 32 : g * 32 + 16, :] = even
         exp_send[g * 32 + 16 : g * 32 + 32, :] = odd
+    sum_counts()
+
+    for _, at in x_peers:
+        push(fx_v.at[core, gx, row], fx_v.at[core, gx, row], fx_sem.at[0], fx_sem.at[1], at)
     for k, at in x_peers:
         push(exp_send.at[rows_of(k, PIECE)], exp_recv.at[rows_of(gx, PIECE)], exp_sem.at[0], exp_sem.at[1], at)
     exp_recv[rows_of(gx, PIECE), :] = exp_send[rows_of(gx, PIECE), :]
 
-    sum_counts()
+    def scale_offset(m, carry):
+        rate_off[m] = off_ref[m] * LOG2E - SHIFT
+        return carry
+
+    lax.fori_loop(0, MARKS, scale_offset, 0)
     send_v[SUMS] = lines(sums_v)
-    for k, at in x_peers:
-        push(send_v.at[SUMS, rows_of(k, 32)], recv_v.at[SUMS, rows_of(gx, 32)], sums_sem.at[0], sums_sem.at[1], at)
-    recv_v[SUMS, rows_of(gx, 32), :] = send_v[SUMS, rows_of(gx, 32), :]
-
     other = {"gy": gy + 1 - 2 * core}
     fy_half = fy_v.at[:, core]
     fy_part = recv_v.at[Y_IN, pl.ds(0, 7 * 32)]
@@ -213,6 +214,10 @@
         arrived(Y_IN, half)
         y_mix(Y_IN, Y_OUT, half, fy_parts)
         exchange(Y_OUT, half, j, y_peers)
+        if half == 0:
+            for k, at in x_peers:
+                push(send_v.at[SUMS, rows_of(k, 32)], recv_v.at[SUMS, rows_of(gx, 32)], sums_sem.at[0], sums_sem.at[1], at)
+            recv_v[SUMS, rows_of(gx, 32), :] = send_v[SUMS, rows_of(gx, 32), :]
 
     fx_eighth = fx_v.at[0, pl.ds(0, N - 1), 0]
     bytes_of(fx_eighth, fx_sem.at[1])
@@ -260,7 +265,7 @@
         def mark(m, total):
             l0 = load_ref[0, m]
             l1 = load_ref[1, m]
-            rate = jnp.exp2(l0 * f0 + (l1 * f1 + (off_ref[m] * LOG2E - SHIFT)))
+            rate = jnp.exp2(l0 * f0 + (l1 * f1 + rate_off[m]))
             return total[0] + l0 * rate, total[1] + l1 * rate
 
         zero = jnp.zeros((GROUP, 128), F32)
@@ -313,6 +318,7 @@
         out_specs=pl.BlockSpec(memory_space=pltpu.VMEM),
         scratch_shapes=[
             pltpu.SMEM((2, MARKS), F32),
+            pltpu.SMEM((MARKS,), F32),
             pltpu.SMEM((MARKS,), F32),
             pltpu.VMEM((2, 32, 1024), F32),
             pltpu.VMEM((32, 1024), F32),

time: 59 us -> 57.4 us (0.973)
  Pallas kernels: 57.2 us -> 55.6 us
    pallas_call x1, Pallas kernels: 57.2 us -> 55.6 us  [body(): pl.pallas_call(kernel, out_shape=jax.ShapeDtypeStruct((2, 32, 1024), F32)...]
where the time goes in v3:
time: 57.4 us; the launch traced here: 57.3 us
  Pallas kernels  55.6 us (97%)
  other arithmetic  1.68 us (3%)
    pallas_call x1, Pallas kernels, body(): pl.pallas_call(kernel, out_shape=jax.ShapeDtypeStruct((2, 32, 1024), F32)...  55.6 us
    sub x1, other arithmetic, body(): return back - whitened  1.68 us

profile of v3, /device:TPU:1, one launch (start us, length us, event | category | flops | bytes accessed | tf_op | source)
XLA Modules:
  0.0 57.3 jit_solution(1743762649185459296)
XLA Ops:
  0.0 0.0 copy-start
  0.0 55.6 %shard_map.82 = f32[2,32,1024]{2,1,0:T(8,128)} custom-call(f32[2,64]{1,0:T(2,128)} %load_hbm.1, f32[64]{0:T(128)} %off_hbm.1, f32[2,32,1024]{2,1,0:T(8,128)} %w_hbm.1, f32[32,512]{1,0:T(8,128)} %fx_hbm.1, f32[16,256]{1,0:T(8,128)} %fy_hbm.1, f32[64,64]{1,0:T(8,128)} %ft_hbm.1, f32[32,1024]{1,0:T(8,128)} %exp_hbm.1, s32[64,32,1024]{2,1,0:T(8,128)} %counts_hbm.1), custom_call_target="tpu_custom_call" | custom-call | tf_op jit(solution)/shard_map/pallas_call | solution.py:314
  55.6 0.0 copy-done
  55.6 1.7 %sub.3 = f32[2,32,1024]{2,1,0:T(8,128)} subtract(f32[2,32,1024]{2,1,0:T(8,128)} %shard_map.82, f32[2,32,1024]{2,1,0:T(8,128)S(1)} %copy-done) | non-fusion elementwise | flops 65536 | bytes 786432 | tf_op jit(solution)/shard_map/sub | solution.py:351
Async XLA Ops:
  0.0 55.6 %copy-start = (f32[2,32,1024]{2,1,0:T(8,128)S(1)}, f32[2,32,1024]{2,1,0:T(8,128)}, u32[]{:S(2)}) copy-start(f32[2,32,1024]{2,1,0:T(8,128)} %w_hbm.1) | copy-start | bytes 786436

commit v4 on v3

--- a/solution.py
+++ b/solution.py
@@ -276,7 +276,7 @@
         rows = slice(k * 16, k * 16 + 16)
         scale = exp_recv[rows, :] * (2.0**SHIFT)
         residual += pack(scale * field_v[0, rows, :], scale * field_v[1, rows, :])
-    back = split(dot(split(recv_v[SUMS] - jnp.concatenate(residual, axis=0)), time))
+    back = split(recv_v[SUMS] - jnp.concatenate(residual, axis=0))
     for half in range(2):
         send_v[X_OUT, pl.ds(half * HALF, HALF), :] = dot_wide((fxt_parts[0, half], fxt_parts[1, half]), back)
         exchange(X_OUT, half, gx, x_peers)
@@ -291,11 +291,13 @@
     for half in range(2):
         arrived(BY_OUT, half)
         xs = slice(half * 16, half * 16 + 16)
+        rows = pl.ds(half * HALF, HALF)
+        t_v[rows, :] = dot(split(recv_v[BY_OUT, rows, :]), time)
         for g in range(8):
             cols = slice(g * 128, g * 128 + 128)
             out_ref[0, xs, cols], out_ref[1, xs, cols] = pack(
-                recv_v[BY_OUT, pl.ds(half * HALF + 2 * g, N, stride=N), :],
-                recv_v[BY_OUT, pl.ds(half * HALF + 2 * g + 1, N, stride=N), :],
+                t_v[pl.ds(half * HALF + 2 * g, N, stride=N), :],
+                t_v[pl.ds(half * HALF + 2 * g + 1, N, stride=N), :],
             )
 
     for phase in range(6):

time: 57.4 us -> 57.3 us (level)
  no operation moved by 1% of the time
where the time goes in v4:
time: 57.3 us; the launch traced here: 57.2 us
  Pallas kernels  55.5 us (97%)
  other arithmetic  1.68 us (3%)
    pallas_call x1, Pallas kernels, body(): pl.pallas_call(kernel, out_shape=jax.ShapeDtypeStruct((2, 32, 1024), F32)...  55.5 us
    sub x1, other arithmetic, body(): return back - whitened  1.68 us

profile of v4, /device:TPU:1, one launch (start us, length us, event | category | flops | bytes accessed | tf_op | source)
XLA Modules:
  0.0 57.2 jit_solution(5135959376832190479)
XLA Ops:
  0.0 0.0 copy-start
  0.0 55.5 %shard_map.82 = f32[2,32,1024]{2,1,0:T(8,128)} custom-call(f32[2,64]{1,0:T(2,128)} %load_hbm.1, f32[64]{0:T(128)} %off_hbm.1, f32[2,32,1024]{2,1,0:T(8,128)} %w_hbm.1, f32[32,512]{1,0:T(8,128)} %fx_hbm.1, f32[16,256]{1,0:T(8,128)} %fy_hbm.1, f32[64,64]{1,0:T(8,128)} %ft_hbm.1, f32[32,1024]{1,0:T(8,128)} %exp_hbm.1, s32[64,32,1024]{2,1,0:T(8,128)} %counts_hbm.1), custom_call_target="tpu_custom_call" | custom-call | tf_op jit(solution)/shard_map/pallas_call | solution.py:316
  55.5 0.0 copy-done
  55.5 1.7 %sub.3 = f32[2,32,1024]{2,1,0:T(8,128)} subtract(f32[2,32,1024]{2,1,0:T(8,128)} %shard_map.82, f32[2,32,1024]{2,1,0:T(8,128)S(1)} %copy-done) | non-fusion elementwise | flops 65536 | bytes 786432 | tf_op jit(solution)/shard_map/sub | solution.py:353
Async XLA Ops:
  0.0 55.5 %copy-start = (f32[2,32,1024]{2,1,0:T(8,128)S(1)}, f32[2,32,1024]{2,1,0:T(8,128)}, u32[]{:S(2)}) copy-start(f32[2,32,1024]{2,1,0:T(8,128)} %w_hbm.1) | copy-start | bytes 786436

commit v5 on v4

--- a/solution.py
+++ b/solution.py
@@ -190,9 +190,9 @@
         exp_send[g * 32 + 16 : g * 32 + 32, :] = odd
     sum_counts()
 
-    for _, at in x_peers:
+    for _, at in x_peers[::-1]:
         push(fx_v.at[core, gx, row], fx_v.at[core, gx, row], fx_sem.at[0], fx_sem.at[1], at)
-    for k, at in x_peers:
+    for k, at in x_peers[::-1]:
         push(exp_send.at[rows_of(k, PIECE)], exp_recv.at[rows_of(gx, PIECE)], exp_sem.at[0], exp_sem.at[1], at)
     exp_recv[rows_of(gx, PIECE), :] = exp_send[rows_of(gx, PIECE), :]
 
@@ -215,7 +215,7 @@
         y_mix(Y_IN, Y_OUT, half, fy_parts)
         exchange(Y_OUT, half, j, y_peers)
         if half == 0:
-            for k, at in x_peers:
+            for k, at in x_peers[::-1]:
                 push(send_v.at[SUMS, rows_of(k, 32)], recv_v.at[SUMS, rows_of(gx, 32)], sums_sem.at[0], sums_sem.at[1], at)
             recv_v[SUMS, rows_of(gx, 32), :] = send_v[SUMS, rows_of(gx, 32), :]
 

time: 57.3 us -> 56.8 us (level)
  no operation moved by 1% of the time
where the time goes in v5:
time: 56.8 us; the launch traced here: 56.7 us
  Pallas kernels  55 us (97%)
  other arithmetic  1.68 us (3%)
    pallas_call x1, Pallas kernels, body(): pl.pallas_call(kernel, out_shape=jax.ShapeDtypeStruct((2, 32, 1024), F32)...  55 us
    sub x1, other arithmetic, body(): return back - whitened  1.68 us

profile of v5, /device:TPU:1, one launch (start us, length us, event | category | flops | bytes accessed | tf_op | source)
XLA Modules:
  0.0 56.7 jit_solution(17470741781670103942)
XLA Ops:
  0.0 0.0 copy-start
  0.0 55.0 %shard_map.82 = f32[2,32,1024]{2,1,0:T(8,128)} custom-call(f32[2,64]{1,0:T(2,128)} %load_hbm.1, f32[64]{0:T(128)} %off_hbm.1, f32[2,32,1024]{2,1,0:T(8,128)} %w_hbm.1, f32[32,512]{1,0:T(8,128)} %fx_hbm.1, f32[16,256]{1,0:T(8,128)} %fy_hbm.1, f32[64,64]{1,0:T(8,128)} %ft_hbm.1, f32[32,1024]{1,0:T(8,128)} %exp_hbm.1, s32[64,32,1024]{2,1,0:T(8,128)} %counts_hbm.1), custom_call_target="tpu_custom_call" | custom-call | tf_op jit(solution)/shard_map/pallas_call | solution.py:316
  55.0 0.0 copy-done
  55.0 1.7 %sub.3 = f32[2,32,1024]{2,1,0:T(8,128)} subtract(f32[2,32,1024]{2,1,0:T(8,128)} %shard_map.82, f32[2,32,1024]{2,1,0:T(8,128)S(1)} %copy-done) | non-fusion elementwise | flops 65536 | bytes 786432 | tf_op jit(solution)/shard_map/sub | solution.py:353
Async XLA Ops:
  0.0 55.0 %copy-start = (f32[2,32,1024]{2,1,0:T(8,128)S(1)}, f32[2,32,1024]{2,1,0:T(8,128)}, u32[]{:S(2)}) copy-start(f32[2,32,1024]{2,1,0:T(8,128)} %w_hbm.1) | copy-start | bytes 786436

commit v6 on v5

--- a/solution.py
+++ b/solution.py
@@ -108,17 +108,14 @@
     def rows_of(k, piece, base=0):
         return pl.ds(pl.multiple_of(base + k * piece, piece), piece)
 
-    def exchange(phase, half, me, peers):
+    def exchange(phase, half, me, peers, load=None):
         mine = rows_of(me, PIECE, half * HALF)
         for k, at in peers:
-            push(
-                send_v.at[phase, rows_of(k, PIECE, half * HALF)],
-                recv_v.at[phase, mine],
-                send_sem.at[phase, half],
-                recv_sem.at[phase, half],
-                at,
-            )
-        recv_v[phase, mine, :] = send_v[phase, mine, :]
+            rows = rows_of(k, PIECE, half * HALF)
+            if load is not None:
+                send_v[phase, rows, :] = load(k)
+            push(send_v.at[phase, rows], recv_v.at[phase, mine], send_sem.at[phase, half], recv_sem.at[phase, half], at)
+        recv_v[phase, mine, :] = send_v[phase, mine, :] if load is None else load(me)
 
     def bytes_of(part, sem):
         pltpu.make_async_copy(part, part, sem).wait()
@@ -282,8 +279,7 @@
         exchange(X_OUT, half, gx, x_peers)
     for half in range(2):
         arrived(X_OUT, half)
-        turn(lambda n: recv_v[X_OUT, pl.ds(half * HALF + n, N, stride=N), :], BY_IN, half)
-        exchange(BY_IN, half, j, y_peers)
+        exchange(BY_IN, half, j, y_peers, lambda n: recv_v[X_OUT, pl.ds(half * HALF + n, N, stride=N), :])
     for half in range(2):
         arrived(BY_IN, half)
         y_mix(BY_IN, BY_OUT, half, (fyt_parts[0], fyt_parts[1]))

time: 56.8 us -> 56.8 us (level)
  no operation moved by 1% of the time
where the time goes in v6:
time: 56.8 us; the launch traced here: 56.7 us
  Pallas kernels  55 us (97%)
  other arithmetic  1.68 us (3%)
    pallas_call x1, Pallas kernels, body(): pl.pallas_call(kernel, out_shape=jax.ShapeDtypeStruct((2, 32, 1024), F32)...  55 us
    sub x1, other arithmetic, body(): return back - whitened  1.68 us

profile of v6, /device:TPU:1, one launch (start us, length us, event | category | flops | bytes accessed | tf_op | source)
XLA Modules:
  0.0 56.7 jit_solution(14809815933443601626)
XLA Ops:
  0.0 0.0 copy-start
  0.0 55.0 %shard_map.82 = f32[2,32,1024]{2,1,0:T(8,128)} custom-call(f32[2,64]{1,0:T(2,128)} %load_hbm.1, f32[64]{0:T(128)} %off_hbm.1, f32[2,32,1024]{2,1,0:T(8,128)} %w_hbm.1, f32[32,512]{1,0:T(8,128)} %fx_hbm.1, f32[16,256]{1,0:T(8,128)} %fy_hbm.1, f32[64,64]{1,0:T(8,128)} %ft_hbm.1, f32[32,1024]{1,0:T(8,128)} %exp_hbm.1, s32[64,32,1024]{2,1,0:T(8,128)} %counts_hbm.1), custom_call_target="tpu_custom_call" | custom-call | tf_op jit(solution)/shard_map/pallas_call | solution.py:312
  55.0 0.0 copy-done
  55.0 1.7 %sub.3 = f32[2,32,1024]{2,1,0:T(8,128)} subtract(f32[2,32,1024]{2,1,0:T(8,128)} %shard_map.82, f32[2,32,1024]{2,1,0:T(8,128)S(1)} %copy-done) | non-fusion elementwise | flops 65536 | bytes 786432 | tf_op jit(solution)/shard_map/sub | solution.py:349
Async XLA Ops:
  0.0 55.0 %copy-start = (f32[2,32,1024]{2,1,0:T(8,128)S(1)}, f32[2,32,1024]{2,1,0:T(8,128)}, u32[]{:S(2)}) copy-start(f32[2,32,1024]{2,1,0:T(8,128)} %w_hbm.1) | copy-start | bytes 786436
